TPU v7x, 32 devices: a whole 2x2x4 slice. The times are simulated.
32 devices in a mesh: pipe: 2 (over core), dp: 16 (over z, y, x).
Axes of the slice: x: 2, y: 2, z: 4, core: 2. Of those that a mesh axis runs over, the one named last changes fastest.
Arguments:
- frames: bfloat16 [32, 8, 49, 2048], P('dp'), may hold values from -6 to 6
- out_grad: bfloat16 [32, 8, 49, 2048], P('dp'), may hold values from -6 to 6
- seg_counts: int32 [32], P('dp'), may hold values from 1 to 8, as said below
- reducer: bfloat16 [2, 2048, 512], P('pipe'), may hold values from -0.125 to 0.125
- spatial: bfloat16 [2, 512, 9, 512], P('pipe'), may hold values from -0.09375 to 0.09375
- expander: bfloat16 [2, 512, 2048], P('pipe'), may hold values from -0.25 to 0.25
- squeezer: bfloat16 [2, 512, 128], P('pipe'), may hold values from -0.25 to 0.25
- motion: bfloat16 [2, 128, 9, 128], P('pipe'), may hold values from -0.1875 to 0.1875
- context: bfloat16 [2, 128, 128], P('pipe'), may hold values from -0.5 to 0.5
- gating: bfloat16 [2, 128, 512], P('pipe'), may hold values from -0.5 to 0.5
- gating_bias: float32 [2, 512], P('pipe'), may hold values from -3 to 3
- norm_params: float32 [2, 2, 3072], P('pipe'), may hold values from -1.5 to 1.5, as said below
Outputs:
- section_out: bfloat16 [2, 32, 8, 49, 2048], P('pipe', 'dp')
- input_grad: bfloat16 [2, 32, 8, 49, 2048], P('pipe', 'dp')
- grad_flat: float32 [2, 4751872], P('pipe', 'dp')
- grad_norms: float32 [2, 2, 3072], P('pipe')
Inputs may be any that keep to these rules, and one draw needn't show every extreme that they name: The first seg_counts[c] segments of clip c are valid and the rest are not; some clip has all 8. `norm_params`: row 0 holds gains, row 1 offsets.
All inputs are finite; a program needn't handle non-finite values.
Results may differ from a plain program's by a relative error of at most 0.02.
Values may be sent and summed in bfloat16 or wider, within the bound.
A program may use at most 256 MiB of HBM per device.

v0:
```python
import jax
import jax.numpy as jnp
from jax import lax
from jax.sharding import PartitionSpec as P

SIDE = 7
PIX = 49
MICRO = 2


EPSILON = 1e-05
HIGH = lax.Precision.HIGHEST


def shifted(x, axis, by):
    length = lax.axis_size(axis)
    pairs = [(i, i + by) for i in range(length) if 0 <= i + by < length]
    return lax.ppermute(x, axis, pairs)


def silu_slope(values):
    sigma = jax.nn.sigmoid(values)
    return sigma * (1.0 + values * (1.0 - sigma))


def take(array, index):
    return lax.dynamic_index_in_dim(array, index, 0, keepdims=False)


def stack_all(*items):
    return jnp.stack(items)


def flatten_grads(items):
    flat = jnp.concatenate([item.reshape(-1) for item in items])
    return flat


def make_patches(values):
    frames_n, pixels, width = values.shape
    maps = values.reshape(frames_n, SIDE, SIDE, width)
    padded = jnp.pad(maps, ((0, 0), (1, 1), (1, 1), (0, 0)))
    patches = jnp.stack(
        [
            padded[:, down : down + SIDE, right : right + SIDE, :]
            for down in range(3)
            for right in range(3)
        ],
        axis=3,
    )
    return patches.reshape(frames_n * pixels, 9, width)


def fold_patches(grads, frames_n, width):
    pieces = grads.reshape(frames_n, SIDE, SIDE, 9, width)
    total = jnp.zeros((frames_n, SIDE + 2, SIDE + 2, width), jnp.float32)
    for down in range(3):
        for right in range(3):
            total = total + jnp.pad(
                pieces[:, :, :, 3 * down + right],
                ((0, 0), (down, 2 - down), (right, 2 - right), (0, 0)),
            )
    return total[:, 1 : SIDE + 1, 1 : SIDE + 1].reshape(frames_n, SIDE * SIDE, width)


def norm_forward(values, mask_pix, count_local):
    total, count = lax.psum((jnp.sum(values * mask_pix, axis=(0, 1)), count_local), "dp")
    mean_value = total / count
    centred = values - mean_value
    spread = lax.psum(jnp.sum(mask_pix * centred * centred, axis=(0, 1)), "dp")
    variance = spread / count
    inverse = lax.rsqrt(variance + EPSILON)
    return (centred * inverse, inverse, count)


def norm_backward(grad_out, normed, inverse, mask_pix, count, gain):
    sum_grad, sum_cross = lax.psum(
        (jnp.sum(grad_out, axis=(0, 1)), jnp.sum(grad_out * normed, axis=(0, 1))), "dp"
    )
    grad_in = gain * inverse * (grad_out - mask_pix * (sum_grad + normed * sum_cross) / count)
    return (grad_in, sum_cross, sum_grad)


def section_forward(inputs, weights, valid, pairs):
    reducer, spatial, expander, squeezer, motion, context, gating, gating_bias, norm_params = (
        weights
    )
    middle_width = reducer.shape[1]
    gains = norm_params[0]
    offsets = norm_params[1]
    frames_n = inputs.shape[0]
    mask_pix = valid[:, None, None]
    count_local = PIX * jnp.sum(valid)
    reduced = jnp.einsum("fpc,co->fpo", inputs, reducer, preferred_element_type=jnp.float32)
    normed_one, inverse_one, count = norm_forward(reduced, mask_pix, count_local)
    first_act = jax.nn.silu(normed_one * gains[:middle_width] + offsets[:middle_width]).astype(
        jnp.bfloat16
    )
    spatial_out = jnp.einsum(
        "pkc,cko->po", make_patches(first_act), spatial, preferred_element_type=jnp.float32
    )
    spatial_out = spatial_out.reshape(frames_n, PIX, middle_width)
    normed_two, inverse_two, unused = norm_forward(spatial_out, mask_pix, count_local)
    middle = jax.nn.silu(
        normed_two * gains[middle_width : 2 * middle_width]
        + offsets[middle_width : 2 * middle_width]
    ).astype(jnp.bfloat16)
    squeezed = jnp.einsum("fpc,co->fpo", middle, squeezer, preferred_element_type=jnp.float32)
    later = jnp.concatenate([squeezed[1:], jnp.zeros_like(squeezed[:1])], axis=0)
    motion_field = (pairs[:, None, None] * (later - squeezed)).astype(jnp.bfloat16)
    context_mean = jnp.mean(motion_field.astype(jnp.float32), axis=1)
    mixed = jnp.einsum(
        "pkc,cko->po", make_patches(motion_field), motion, preferred_element_type=jnp.float32
    )
    mixed = (
        mixed.reshape(frames_n, PIX, -1)
        + jnp.dot(context_mean, context.astype(jnp.float32), precision=HIGH)[:, None, :]
    )
    scores = mixed.astype(jnp.bfloat16)
    logits = (
        jnp.einsum("fpc,co->fpo", scores, gating, preferred_element_type=jnp.float32) + gating_bias
    )
    sigma = jax.nn.sigmoid(logits)
    gated = (middle.astype(jnp.float32) * (0.5 + sigma)).astype(jnp.bfloat16)
    expanded = jnp.einsum("fpc,co->fpo", gated, expander, preferred_element_type=jnp.float32)
    normed_three, inverse_three, unused = norm_forward(expanded, mask_pix, count_local)
    summed = (
        inputs.astype(jnp.float32)
        + normed_three * gains[2 * middle_width :]
        + offsets[2 * middle_width :]
    )
    output = (mask_pix * jax.nn.silu(summed)).astype(jnp.bfloat16)
    saved = (
        inputs,
        normed_one,
        inverse_one,
        first_act,
        normed_two,
        inverse_two,
        middle,
        motion_field,
        context_mean,
        scores,
        sigma,
        gated,
        normed_three,
        inverse_three,
        count,
    )
    return (output, saved)


def section_backward(grad_output, saved, weights, valid, pairs):
    reducer, spatial, expander, squeezer, motion, context, gating, gating_bias, norm_params = (
        weights
    )
    (
        inputs,
        normed_one,
        inverse_one,
        first_act,
        normed_two,
        inverse_two,
        middle,
        motion_field,
        context_mean,
        scores,
        sigma,
        gated,
        normed_three,
        inverse_three,
        count,
    ) = saved
    middle_width = reducer.shape[1]
    gains = norm_params[0]
    offsets = norm_params[1]
    frames_n = inputs.shape[0]
    mask_pix = valid[:, None, None]
    gain_three = gains[2 * middle_width :]
    summed = inputs.astype(jnp.float32) + normed_three * gain_three + offsets[2 * middle_width :]
    grad_summed = grad_output.astype(jnp.float32) * mask_pix * silu_slope(summed)
    grad_expanded, gain_three_grad, offset_three_grad = norm_backward(
        grad_summed, normed_three, inverse_three, mask_pix, count, gain_three
    )
    grad_expanded = grad_expanded.astype(jnp.bfloat16)
    expander_grad = jnp.einsum(
        "fpc,fpo->co", gated, grad_expanded, preferred_element_type=jnp.float32
    )
    grad_gated = jnp.einsum(
        "fpo,co->fpc", grad_expanded, expander, preferred_element_type=jnp.float32
    )
    grad_middle = grad_gated * (0.5 + sigma)
    grad_logits = (grad_gated * middle.astype(jnp.float32) * sigma * (1.0 - sigma)).astype(
        jnp.bfloat16
    )
    gating_grad = jnp.einsum("fpc,fpo->co", scores, grad_logits, preferred_element_type=jnp.float32)
    bias_grad = jnp.sum(grad_logits.astype(jnp.float32), axis=(0, 1))
    grad_scores = jnp.einsum(
        "fpo,co->fpc", grad_logits, gating, preferred_element_type=jnp.float32
    ).astype(jnp.bfloat16)
    score_rows = grad_scores.reshape(frames_n * PIX, -1)
    motion_grad = jnp.einsum(
        "pkc,po->cko", make_patches(motion_field), score_rows, preferred_element_type=jnp.float32
    )
    grad_motion_field = fold_patches(
        jnp.einsum("po,cko->pkc", score_rows, motion, preferred_element_type=jnp.float32),
        frames_n,
        motion.shape[0],
    )
    score_sums = jnp.sum(grad_scores.astype(jnp.float32), axis=1)
    context_grad = jnp.dot(context_mean.T, score_sums, precision=HIGH)
    grad_motion_field = (
        grad_motion_field
        + (jnp.dot(score_sums, context.astype(jnp.float32).T, precision=HIGH) / PIX)[:, None, :]
    )
    weighted = pairs[:, None, None] * grad_motion_field
    grad_squeezed = (
        jnp.concatenate([jnp.zeros_like(weighted[:1]), weighted[:-1]], axis=0) - weighted
    ).astype(jnp.bfloat16)
    squeezer_grad = jnp.einsum(
        "fpc,fpo->co", middle, grad_squeezed, preferred_element_type=jnp.float32
    )
    grad_middle = grad_middle + jnp.einsum(
        "fpo,co->fpc", grad_squeezed, squeezer, preferred_element_type=jnp.float32
    )
    gain_two = gains[middle_width : 2 * middle_width]
    before_two = normed_two * gain_two + offsets[middle_width : 2 * middle_width]
    grad_spatial_out, gain_two_grad, offset_two_grad = norm_backward(
        grad_middle * silu_slope(before_two), normed_two, inverse_two, mask_pix, count, gain_two
    )
    spatial_rows = grad_spatial_out.astype(jnp.bfloat16).reshape(frames_n * PIX, middle_width)
    spatial_grad = jnp.einsum(
        "pkc,po->cko", make_patches(first_act), spatial_rows, preferred_element_type=jnp.float32
    )
    grad_first = fold_patches(
        jnp.einsum("po,cko->pkc", spatial_rows, spatial, preferred_element_type=jnp.float32),
        frames_n,
        middle_width,
    )
    gain_one = gains[:middle_width]
    before_one = normed_one * gain_one + offsets[:middle_width]
    grad_reduced, gain_one_grad, offset_one_grad = norm_backward(
        grad_first * silu_slope(before_one), normed_one, inverse_one, mask_pix, count, gain_one
    )
    grad_reduced = grad_reduced.astype(jnp.bfloat16)
    reducer_grad = jnp.einsum(
        "fpc,fpo->co", inputs, grad_reduced, preferred_element_type=jnp.float32
    )
    grad_inputs = (
        grad_summed
        + jnp.einsum("fpo,co->fpc", grad_reduced, reducer, preferred_element_type=jnp.float32)
    ).astype(jnp.bfloat16)
    weight_grads = (
        reducer_grad,
        spatial_grad,
        expander_grad,
        squeezer_grad,
        motion_grad,
        context_grad,
        gating_grad,
        bias_grad,
    )
    norm_grads = jnp.stack(
        [
            jnp.concatenate([gain_one_grad, gain_two_grad, gain_three_grad]),
            jnp.concatenate([offset_one_grad, offset_two_grad, offset_three_grad]),
        ]
    )
    return (grad_inputs, weight_grads, norm_grads)


def on_device(
    frames,
    out_grad,
    seg_counts,
    reducer,
    spatial,
    expander,
    squeezer,
    motion,
    context,
    gating,
    gating_bias,
    norm_params,
):
    weights = (
        reducer[0],
        spatial[0],
        expander[0],
        squeezer[0],
        motion[0],
        context[0],
        gating[0],
        gating_bias[0],
        norm_params[0],
    )
    section = lax.axis_index("pipe")
    clips_dev, segs, pixels, width = frames.shape
    per_micro = clips_dev // MICRO
    shape_mb = (MICRO, per_micro * segs, pixels, width)
    segment = jnp.arange(segs, dtype=jnp.int32)
    counts_mb = seg_counts.reshape(MICRO, per_micro, 1)
    valid_mb = (segment < counts_mb).astype(jnp.float32).reshape(MICRO, per_micro * segs)
    pairs_mb = (segment + 1 < counts_mb).astype(jnp.float32).reshape(MICRO, per_micro * segs)
    arriving = jnp.zeros(shape_mb[1:], jnp.bfloat16)
    outputs = jnp.zeros(shape_mb, jnp.bfloat16)
    saved_list = []
    for tick in range(MICRO + 1):
        micro = tick - section
        index = jnp.clip(micro, 0, MICRO - 1)
        active = jnp.logical_and(micro >= 0, micro < MICRO)
        inputs = jnp.where(section == 0, take(frames, index), arriving)
        output, saved = section_forward(
            inputs, weights, take(valid_mb, index), take(pairs_mb, index)
        )
        saved_list.append(saved)
        outputs = lax.dynamic_update_index_in_dim(
            outputs, jnp.where(active, output, take(outputs, index)), index, 0
        )
        if tick < MICRO:
            arriving = shifted(output, "pipe", 1)
    stacked = jax.tree.map(stack_all, *saved_list)
    likes = weights[:8]
    totals = tuple((jnp.zeros(item.shape, jnp.float32) for item in likes))
    norm_total = jnp.zeros((2, norm_params.shape[-1]), jnp.float32)
    arriving_back = jnp.zeros(shape_mb[1:], jnp.bfloat16)
    input_grads = jnp.zeros(shape_mb, jnp.bfloat16)
    for tick in range(MICRO + 1):
        micro = tick - 1 + section
        index = jnp.clip(micro, 0, MICRO - 1)
        active = jnp.logical_and(micro >= 0, micro < MICRO)
        forward_tick = jnp.clip(micro + section, 0, MICRO)
        saved = jax.tree.map(lambda item: take(item, forward_tick), stacked)
        grad_output = jnp.where(section == 1, take(out_grad, index), arriving_back)
        grad_inputs, weight_grads, norm_grads = section_backward(
            grad_output, saved, weights, take(valid_mb, index), take(pairs_mb, index)
        )
        scale = active.astype(jnp.float32)
        scaled = tuple((item * scale for item in weight_grads))
        totals = tuple((old + new for old, new in zip(totals, scaled)))
        norm_total = norm_total + norm_grads * scale
        input_grads = lax.dynamic_update_index_in_dim(
            input_grads, jnp.where(active, grad_inputs, take(input_grads, index)), index, 0
        )
        if tick < MICRO:
            arriving_back = shifted(grad_inputs, "pipe", -1)
    share = lax.psum_scatter(flatten_grads(totals), "dp", scatter_dimension=0, tiled=True)
    return (outputs[None], input_grads[None], share[None], norm_total[None])


def solution(mesh):
    in_specs = (
        P("dp", None, None, None),
        P("dp", None, None, None),
        P("dp"),
        P("pipe", None, None),
        P("pipe", None, None, None),
        P("pipe", None, None),
        P("pipe", None, None),
        P("pipe", None, None, None),
        P("pipe", None, None),
        P("pipe", None, None),
        P("pipe", None),
        P("pipe", None, None),
    )
    out_specs = (
        P("pipe", "dp", None, None, None),
        P("pipe", "dp", None, None, None),
        P("pipe", "dp"),
        P("pipe", None, None),
    )
    return jax.shard_map(
        on_device, mesh=mesh, in_specs=in_specs, out_specs=out_specs, check_vma=False
    )
```

profile of v0, /device:TPU:4, one launch (start us, length us, event | category | flops | bytes accessed | tf_op | source)
XLA Modules:
  0.0 2682.2 jit_solution(17475060863979670399)
XLA Ops:
  18.3 39.0 %all-reduce.84 = (f32[512]{0:T(512)S(1)}, f32[]{:T(128)}) all-reduce(f32[512]{0:T(512)S(1)} %get-tuple-element.283, f32[]{:T(128)S(6)} %mul.1211), channel_id=1, replica_groups=mesh['pipe'=2,'dp'=16] {'dp'}, use_global_device_ids=true, to_apply=%region_1.2 | all-reduce | flops 513 | bytes 4104 | tf_op jit(solution)/shard_map/psum | solution.py:67
  58.2 36.6 %psum.293 = f32[512]{0:T(512)S(1)} all-reduce(f32[512]{0:T(512)S(1)} %fusion.143), channel_id=1, replica_groups=mesh['pipe'=2,'dp'=16] {'dp'}, use_global_device_ids=true, to_apply=%region_5.6 | all-reduce | flops 512 | bytes 4096 | tf_op jit(solution)/shard_map/psum | solution.py:70
  143.3 38.6 %psum.294 = f32[512]{0:T(512)S(1)} all-reduce(f32[512]{0:T(512)S(1)} %get-tuple-element.285), channel_id=1, replica_groups=mesh['pipe'=2,'dp'=16] {'dp'}, use_global_device_ids=true, to_apply=%region_7.8 | all-reduce | flops 512 | bytes 4096 | tf_op jit(solution)/shard_map/psum | solution.py:67
  183.9 37.0 %psum.295 = f32[512]{0:T(512)S(1)} all-reduce(f32[512]{0:T(512)S(1)} %fusion.144), channel_id=1, replica_groups=mesh['pipe'=2,'dp'=16] {'dp'}, use_global_device_ids=true, to_apply=%region_9.10 | all-reduce | flops 512 | bytes 4096 | tf_op jit(solution)/shard_map/psum | solution.py:70
  277.4 39.8 %psum.296 = f32[2048]{0:T(1024)} all-reduce(f32[2048]{0:T(1024)} %get-tuple-element.287), channel_id=1, replica_groups=mesh['pipe'=2,'dp'=16] {'dp'}, use_global_device_ids=true, to_apply=%region_12.13 | all-reduce | flops 2048 | bytes 16384 | tf_op jit(solution)/shard_map/psum | solution.py:67
  322.2 37.8 %psum.297 = f32[2048]{0:T(1024)} all-reduce(f32[2048]{0:T(1024)} %fusion.24), channel_id=1, replica_groups=mesh['pipe'=2,'dp'=16] {'dp'}, use_global_device_ids=true, to_apply=%region_14.15 | all-reduce | flops 2048 | bytes 16384 | tf_op jit(solution)/shard_map/psum | solution.py:70
  394.9 39.1 %all-reduce.83 = (f32[512]{0:T(512)S(1)}, f32[]{:T(128)}) all-reduce(f32[512]{0:T(512)S(1)} %get-tuple-element.289, f32[]{:T(128)S(6)} %mul.1247), channel_id=1, replica_groups=mesh['pipe'=2,'dp'=16] {'dp'}, use_global_device_ids=true, to_apply=%region_16.17 | all-reduce | flops 513 | bytes 4104 | tf_op jit(solution)/shard_map/psum | solution.py:67
  436.5 36.8 %psum.300 = f32[512]{0:T(512)S(1)} all-reduce(f32[512]{0:T(512)S(1)} %fusion.145), channel_id=1, replica_groups=mesh['pipe'=2,'dp'=16] {'dp'}, use_global_device_ids=true, to_apply=%region_20.21 | all-reduce | flops 512 | bytes 4096 | tf_op jit(solution)/shard_map/psum | solution.py:70
  525.5 38.5 %psum.301 = f32[512]{0:T(512)S(1)} all-reduce(f32[512]{0:T(512)S(1)} %get-tuple-element.291), channel_id=1, replica_groups=mesh['pipe'=2,'dp'=16] {'dp'}, use_global_device_ids=true, to_apply=%region_22.23 | all-reduce | flops 512 | bytes 4096 | tf_op jit(solution)/shard_map/psum | solution.py:67
  566.6 36.6 %psum.302 = f32[512]{0:T(512)S(1)} all-reduce(f32[512]{0:T(512)S(1)} %fusion.146), channel_id=1, replica_groups=mesh['pipe'=2,'dp'=16] {'dp'}, use_global_device_ids=true, to_apply=%region_24.25 | all-reduce | flops 512 | bytes 4096 | tf_op jit(solution)/shard_map/psum | solution.py:70
  660.6 39.7 %psum.303 = f32[2048]{0:T(1024)} all-reduce(f32[2048]{0:T(1024)} %get-tuple-element.293), channel_id=1, replica_groups=mesh['pipe'=2,'dp'=16] {'dp'}, use_global_device_ids=true, to_apply=%region_27.28 | all-reduce | flops 2048 | bytes 16384 | tf_op jit(solution)/shard_map/psum | solution.py:67
  705.4 38.3 %psum.304 = f32[2048]{0:T(1024)} all-reduce(f32[2048]{0:T(1024)} %fusion.25), channel_id=1, replica_groups=mesh['pipe'=2,'dp'=16] {'dp'}, use_global_device_ids=true, to_apply=%region_29.30 | all-reduce | flops 2048 | bytes 16384 | tf_op jit(solution)/shard_map/psum | solution.py:70
  766.8 39.0 %all-reduce.82 = (f32[512]{0:T(512)S(1)}, f32[]{:T(128)}) all-reduce(f32[512]{0:T(512)S(1)} %get-tuple-element.295, f32[]{:T(128)S(6)} %mul.1277), channel_id=1, replica_groups=mesh['pipe'=2,'dp'=16] {'dp'}, use_global_device_ids=true, to_apply=%region_31.32 | all-reduce | flops 513 | bytes 4104 | tf_op jit(solution)/shard_map/psum | solution.py:67
  808.3 36.9 %psum.307 = f32[512]{0:T(512)S(1)} all-reduce(f32[512]{0:T(512)S(1)} %fusion.147), channel_id=1, replica_groups=mesh['pipe'=2,'dp'=16] {'dp'}, use_global_device_ids=true, to_apply=%region_35.36 | all-reduce | flops 512 | bytes 4096 | tf_op jit(solution)/shard_map/psum | solution.py:70
  897.3 38.4 %psum.308 = f32[512]{0:T(512)S(1)} all-reduce(f32[512]{0:T(512)S(1)} %get-tuple-element.297), channel_id=1, replica_groups=mesh['pipe'=2,'dp'=16] {'dp'}, use_global_device_ids=true, to_apply=%region_37.38 | all-reduce | flops 512 | bytes 4096 | tf_op jit(solution)/shard_map/psum | solution.py:67
  938.3 36.7 %psum.309 = f32[512]{0:T(512)S(1)} all-reduce(f32[512]{0:T(512)S(1)} %fusion.148), channel_id=1, replica_groups=mesh['pipe'=2,'dp'=16] {'dp'}, use_global_device_ids=true, to_apply=%region_39.40 | all-reduce | flops 512 | bytes 4096 | tf_op jit(solution)/shard_map/psum | solution.py:70
  1042.3 39.3 %psum.310 = f32[2048]{0:T(1024)S(1)} all-reduce(f32[2048]{0:T(1024)S(1)} %get-tuple-element.299), channel_id=1, replica_groups=mesh['pipe'=2,'dp'=16] {'dp'}, use_global_device_ids=true, to_apply=%region_42.43 | all-reduce | flops 2048 | bytes 16384 | tf_op jit(solution)/shard_map/psum | solution.py:67
  1084.8 37.2 %psum.311 = f32[2048]{0:T(1024)S(1)} all-reduce(f32[2048]{0:T(1024)S(1)} %fusion.26), channel_id=1, replica_groups=mesh['pipe'=2,'dp'=16] {'dp'}, use_global_device_ids=true, to_apply=%region_44.45 | all-reduce | flops 2048 | bytes 16384 | tf_op jit(solution)/shard_map/psum | solution.py:70
  1138.8 11.4 pad_maximum_fusion
  1157.5 73.4 %all-reduce.81 = (f32[2048]{0:T(1024)S(1)}, f32[2048]{0:T(1024)S(1)}) all-reduce(f32[2048]{0:T(1024)S(1)} %get-tuple-element.9, f32[2048]{0:T(1024)S(1)} %get-tuple-element.8), channel_id=1, replica_groups=mesh['pipe'=2,'dp'=16] {'dp'}, use_global_device_ids=true, to_apply=%region_48.49 | all-reduce | flops 4096 | bytes 32768 | tf_op jit(solution)/shard_map/psum | solution.py:77
  1257.5 36.7 %all-reduce.80 = (f32[512]{0:T(512)S(1)}, f32[512]{0:T(512)S(1)}) all-reduce(f32[512]{0:T(512)S(1)} %get-tuple-element.15, f32[512]{0:T(512)S(1)} %get-tuple-element.14), channel_id=1, replica_groups=mesh['pipe'=2,'dp'=16] {'dp'}, use_global_device_ids=true, to_apply=%region_53.54 | all-reduce | flops 1024 | bytes 8192 | tf_op jit(solution)/shard_map/psum | solution.py:77
  1325.8 38.5 %all-reduce.79 = (f32[512]{0:T(512)S(1)}, f32[512]{0:T(512)S(1)}) all-reduce(f32[512]{0:T(512)S(1)} %fusion.178, f32[512]{0:T(512)S(1)} %get-tuple-element.55), channel_id=1, replica_groups=mesh['pipe'=2,'dp'=16] {'dp'}, use_global_device_ids=true, to_apply=%region_57.58 | all-reduce | flops 1024 | bytes 8192 | tf_op jit(solution)/shard_map/psum | solution.py:77
  1633.1 71.7 %all-reduce.78 = (f32[2048]{0:T(1024)S(1)}, f32[2048]{0:T(1024)S(1)}) all-reduce(f32[2048]{0:T(1024)S(1)} %get-tuple-element.7, f32[2048]{0:T(1024)S(1)} %get-tuple-element.6), channel_id=1, replica_groups=mesh['pipe'=2,'dp'=16] {'dp'}, use_global_device_ids=true, to_apply=%region_61.62 | all-reduce | flops 4096 | bytes 32768 | tf_op jit(solution)/shard_map/psum | solution.py:77
  1729.0 36.9 %all-reduce.77 = (f32[512]{0:T(512)S(1)}, f32[512]{0:T(512)S(1)}) all-reduce(f32[512]{0:T(512)S(1)} %get-tuple-element.13, f32[512]{0:T(512)S(1)} %get-tuple-element.12), channel_id=1, replica_groups=mesh['pipe'=2,'dp'=16] {'dp'}, use_global_device_ids=true, to_apply=%region_66.67 | all-reduce | flops 1024 | bytes 8192 | tf_op jit(solution)/shard_map/psum | solution.py:77
  1798.2 38.6 %all-reduce.76 = (f32[512]{0:T(512)S(1)}, f32[512]{0:T(512)S(1)}) all-reduce(f32[512]{0:T(512)S(1)} %fusion.164, f32[512]{0:T(512)S(1)} %get-tuple-element.52), channel_id=1, replica_groups=mesh['pipe'=2,'dp'=16] {'dp'}, use_global_device_ids=true, to_apply=%region_70.71 | all-reduce | flops 1024 | bytes 8192 | tf_op jit(solution)/shard_map/psum | solution.py:77
  1864.7 10.9 fusion.332
  1875.7 71.7 %all-reduce.75 = (f32[2048]{0:T(1024)S(1)}, f32[2048]{0:T(1024)S(1)}) all-reduce(f32[2048]{0:T(1024)S(1)} %get-tuple-element.5, f32[2048]{0:T(1024)S(1)} %get-tuple-element.4), channel_id=1, replica_groups=mesh['pipe'=2,'dp'=16] {'dp'}, use_global_device_ids=true, to_apply=%region_74.75 | all-reduce | flops 4096 | bytes 32768 | tf_op jit(solution)/shard_map/psum | solution.py:77
  1971.1 36.5 %all-reduce.74 = (f32[512]{0:T(512)S(1)}, f32[512]{0:T(512)S(1)}) all-reduce(f32[512]{0:T(512)S(1)} %get-tuple-element.11, f32[512]{0:T(512)S(1)} %get-tuple-element.10), channel_id=1, replica_groups=mesh['pipe'=2,'dp'=16] {'dp'}, use_global_device_ids=true, to_apply=%region_79.80 | all-reduce | flops 1024 | bytes 8192 | tf_op jit(solution)/shard_map/psum | solution.py:77
  2065.4 16.7 copy.514
  2082.1 13.9 reshape.768
  2096.0 38.5 %all-reduce.73 = (f32[512]{0:T(512)S(1)}, f32[512]{0:T(512)S(1)}) all-reduce(f32[512]{0:T(512)S(1)} %fusion.150, f32[512]{0:T(512)S(1)} %get-tuple-element.49), channel_id=1, replica_groups=mesh['pipe'=2,'dp'=16] {'dp'}, use_global_device_ids=true, to_apply=%region_83.84 | all-reduce | flops 1024 | bytes 8192 | tf_op jit(solution)/shard_map/psum | solution.py:77
  2181.5 485.7 %all-reduce.87.cloned.1.call-done = f32[4751872]{0:T(1024)} async-done(((f32[4751872]{0:T(1024)}), f32[4751872]{0:T(1024)}) %all-reduce.87.cloned.1.call-update) | async-done | bytes 19007504
  (1169 shorter events, 995.3 us)
Async XLA Ops:
  7.2 266.5 %copy-start = (bf16[1,512,2048]{2,1,0:T(8,128)(2,1)S(1)}, bf16[1,512,2048]{2,1,0:T(8,128)(2,1)}, u32[]{:S(2)}) copy-start(bf16[1,512,2048]{2,1,0:T(8,128)(2,1)} %param.17) | copy-start | bytes 6291460
  7.2 2660.1 %all-reduce.87.cloned.1.call-start = ((), (), s32[]{:S(2)}) async-start(), calls=%async_computation | async-start | bytes 38019072
  14.2 168.4 %copy-start.222 = (f32[8]{0:T(128)}, f32[8]{0:T(128)S(1)}, u32[]{:S(2)}) copy-start(f32[8]{0:T(128)S(1)} %get-tuple-element.277) | copy-start | bytes 100
  18.3 77.9 %copy-start.60 = (f32[8,49,512]{2,1,0:T(8,128)}, f32[8,49,512]{2,1,0:T(8,128)S(1)}, u32[]{:S(2)}) copy-start(f32[8,49,512]{2,1,0:T(8,128)S(1)} %get-tuple-element.284) | copy-start | bytes 2408452
  96.2 125.4 %copy-start.183 = (f32[1,1,512]{2,1,0:T(1,128)}, f32[1,1,512]{2,1,0:T(1,128)S(1)}, u32[]{:S(2)}) copy-start(f32[1,1,512]{2,1,0:T(1,128)S(1)} %get-tuple-element.260) | copy-start | bytes 6148
  96.2 125.4 %copy-start.186 = (f32[1,1,512]{2,1,0:T(1,128)}, f32[1,1,512]{2,1,0:T(1,128)S(1)}, u32[]{:S(2)}) copy-start(f32[1,1,512]{2,1,0:T(1,128)S(1)} %get-tuple-element.261) | copy-start | bytes 6148
  136.5 87.6 %copy-start.126 = (bf16[1,512,128]{2,1,0:T(8,128)(2,1)S(1)}, bf16[1,512,128]{2,1,0:T(8,128)(2,1)}, u32[]{:S(2)}) copy-start(bf16[1,512,128]{2,1,0:T(8,128)(2,1)} %param.18) | copy-start | bytes 393220
  143.3 83.1 %copy-start.174 = (f32[1,2,3072]{2,1,0:T(2,128)S(1)}, f32[1,2,3072]{2,1,0:T(2,128)}, u32[]{:S(2)}) copy-start(f32[1,2,3072]{2,1,0:T(2,128)} %param.23) | copy-start | bytes 73732
  224.0 146.9 %copy-start.22 = (bf16[8,49,512]{2,1,0:T(8,128)(2,1)}, bf16[8,49,512]{2,1,0:T(8,128)(2,1)S(1)}, u32[]{:S(2)}) copy-start(bf16[8,49,512]{2,1,0:T(8,128)(2,1)S(1)} %get-tuple-element.138) | copy-start | bytes 1204228
  228.0 41.1 %copy-start.26 = (bf16[1,128,9,128]{3,1,2,0:T(8,128)(2,1)S(1)}, bf16[1,128,9,128]{3,1,2,0:T(8,128)(2,1)}, u32[]{:S(2)}) copy-start(bf16[1,128,9,128]{3,1,2,0:T(8,128)(2,1)} %param.19) | copy-start | bytes 884740
  368.4 20.3 collective-permute-start
  606.3 151.9 %copy-start.23 = (bf16[8,49,512]{2,1,0:T(8,128)(2,1)}, bf16[8,49,512]{2,1,0:T(8,128)(2,1)S(1)}, u32[]{:S(2)}) copy-start(bf16[8,49,512]{2,1,0:T(8,128)(2,1)S(1)} %get-tuple-element.140) | copy-start | bytes 1204228
  607.4 44.0 %copy-start.182 = (f32[8,128]{1,0:T(8,128)}, f32[8,128]{1,0:T(8,128)S(1)}, u32[]{:S(2)}) copy-start(f32[8,128]{1,0:T(8,128)S(1)} %get-tuple-element.62) | copy-start | bytes 12292
  660.6 84.4 %copy-start.144 = (f32[1,1,2048]{2,1,0:T(1,128)S(1)}, f32[1,1,2048]{2,1,0:T(1,128)}, u32[]{:S(2)}) copy-start(f32[1,1,2048]{2,1,0:T(1,128)} %get-tuple-element.264) | copy-start | bytes 24580
  660.6 84.4 %copy-start.145 = (f32[1,1,2048]{2,1,0:T(1,128)S(1)}, f32[1,1,2048]{2,1,0:T(1,128)}, u32[]{:S(2)}) copy-start(f32[1,1,2048]{2,1,0:T(1,128)} %get-tuple-element.265) | copy-start | bytes 24580
  754.2 8.1 collective-permute-start.1
  978.1 57.6 %copy-start.24 = (bf16[8,49,512]{2,1,0:T(8,128)(2,1)}, bf16[8,49,512]{2,1,0:T(8,128)(2,1)S(1)}, u32[]{:S(2)}) copy-start(bf16[8,49,512]{2,1,0:T(8,128)(2,1)S(1)} %get-tuple-element.142) | copy-start | bytes 1204228
  1253.1 41.1 %copy-start.233 = (f32[8]{0:T(128)S(1)}, f32[8]{0:T(128)}, u32[]{:S(2)}) copy-start(f32[8]{0:T(128)} %get-tuple-element.274) | copy-start | bytes 100
  1374.3 252.5 %collective-permute-start.2 = (bf16[8,49,2048]{2,0,1:T(8,128)(2,1)}, bf16[8,49,2048]{2,0,1:T(8,128)(2,1)}, u32[]{:S(2)}, u32[]{:S(2)}) collective-permute-start(bf16[8,49,2048]{2,0,1:T(8,128)(2,1)} %copy.447), channel_id=1, source_target_pairs={{16,0},{17,1},{18,2},{19,3},{20,4},{21,5},{22,6},{23,7},{24,8},{25... | collective-permute-start | bytes 4816904 | tf_op jit(solution)/shard_map/ppermute | solution.py:18
  1564.2 37.3 %copy-start.94 = (bf16[392,1,512]{2,0,1:T(8,128)(2,1)S(1)}, bf16[392,1,512]{2,0,1:T(8,128)(2,1)}, u32[]{:S(2)}) copy-start(bf16[392,1,512]{2,0,1:T(8,128)(2,1)} %stack.684) | copy-start | bytes 1204228
  1564.2 37.4 %copy-start.96 = (bf16[392,1,512]{2,0,1:T(8,128)(2,1)S(1)}, bf16[392,1,512]{2,0,1:T(8,128)(2,1)}, u32[]{:S(2)}) copy-start(bf16[392,1,512]{2,0,1:T(8,128)(2,1)} %stack.685) | copy-start | bytes 1204228
  1564.2 37.4 %copy-start.91 = (bf16[392,1,512]{2,0,1:T(8,128)(2,1)S(1)}, bf16[392,1,512]{2,0,1:T(8,128)(2,1)}, u32[]{:S(2)}) copy-start(bf16[392,1,512]{2,0,1:T(8,128)(2,1)} %stack.686) | copy-start | bytes 1204228
  1564.2 37.4 %copy-start.176 = (f32[3,8,128]{2,1,0:T(8,128)}, f32[3,8,128]{2,1,0:T(8,128)S(1)}, u32[]{:S(2)}) copy-start(f32[3,8,128]{2,1,0:T(8,128)S(1)} %pad_maximum_fusion.11) | copy-start | bytes 36868
  1725.4 40.6 %copy-start.253 = (f32[1,1,512]{2,1,0:T(1,128)S(1)}, f32[1,1,512]{2,1,0:T(1,128)}, u32[]{:S(2)}) copy-start(f32[1,1,512]{2,1,0:T(1,128)} %get-tuple-element.258) | copy-start | bytes 6148
  1796.3 40.4 %copy-start.252 = (f32[1,1,512]{2,1,0:T(1,128)S(1)}, f32[1,1,512]{2,1,0:T(1,128)}, u32[]{:S(2)}) copy-start(f32[1,1,512]{2,1,0:T(1,128)} %get-tuple-element.252) | copy-start | bytes 6148
  1844.3 20.4 collective-permute-start.3
  1864.7 82.7 %copy-start.189 = (f32[1,1,2048]{2,1,0:T(1,128)S(1)}, f32[1,1,2048]{2,1,0:T(1,128)}, u32[]{:S(2)}) copy-start(f32[1,1,2048]{2,1,0:T(1,128)} %get-tuple-element.248) | copy-start | bytes 24580
  1968.0 39.6 %copy-start.229 = (f32[8]{0:T(128)S(1)}, f32[8]{0:T(128)}, u32[]{:S(2)}) copy-start(f32[8]{0:T(128)} %get-tuple-element.272) | copy-start | bytes 100
  1968.0 39.6 %copy-start.251 = (f32[1,1,512]{2,1,0:T(1,128)S(1)}, f32[1,1,512]{2,1,0:T(1,128)}, u32[]{:S(2)}) copy-start(f32[1,1,512]{2,1,0:T(1,128)} %get-tuple-element.259) | copy-start | bytes 6148
  2082.1 52.5 %copy-start.43 = (f32[1,8,49,512]{3,1,2,0:T(8,128)S(1)}, f32[1,8,49,512]{3,1,2,0:T(8,128)}, u32[]{:S(2)}) copy-start(f32[1,8,49,512]{3,1,2,0:T(8,128)} %copy.479) | copy-start | bytes 2408452
  2082.1 52.5 %copy-start.230 = (f32[8]{0:T(128)S(1)}, f32[8]{0:T(128)}, u32[]{:S(2)}) copy-start(f32[8]{0:T(128)} %get-tuple-element.272) | copy-start | bytes 100
  2082.1 52.5 %copy-start.250 = (f32[1,1,512]{2,1,0:T(1,128)S(1)}, f32[1,1,512]{2,1,0:T(1,128)}, u32[]{:S(2)}) copy-start(f32[1,1,512]{2,1,0:T(1,128)} %get-tuple-element.251) | copy-start | bytes 6148
  (249 other events, 1435.6 us)
Sparse Core Ops, SparseCore 0:
  2159.2 507.9 all-reduce.86
where the time goes:
time: 2700 us; the launch traced here: 2680 us
  blocking collectives  1130 us (42%)
  local copies, waits for them, and re-layouts  690 us (26%)
  waiting for transfers between devices  486 us (18%)
  matrix products  177 us (7%)
  other arithmetic  173 us (6%)
    unnamed x2, waiting for transfers between devices  486 us
    psum x9, blocking collectives, norm_backward(): lax.psum((jnp.sum(grad_out, axis=(0, 1)), jnp.sum(grad_out * normed, axis...  443 us
    psum x9, blocking collectives, norm_forward(): lax.psum((jnp.sum(values * mask_pix, axis=(0, 1)), count_local), 'dp')  351 us
    psum x9, blocking collectives, norm_forward(): spread = lax.psum(jnp.sum(mask_pix * centred * centred, axis=(0, 1)), 'dp')  334 us
    unnamed x685, local copies, waits for them, and re-layouts  182 us
    slice x108, local copies, waits for them, and re-layouts, make_patches(): padded[:, down:down + SIDE, right:right + SIDE, :]  167 us
    another operation x120, local copies, waits for them, and re-layouts, make_patches(): jnp.stack([padded[:, down:down + SIDE, right:right + SIDE, :] for down in...  166 us
  transfers between devices with their start and end apart: 5, of which 1 were waited for; matrix products, arithmetic and copies ran while one was open for 11% of the time, Pallas kernels for 0%

commit v1 on v0

v1 whole, which is shorter than its diff:
```python
import functools
from types import SimpleNamespace

import jax
import jax.numpy as jnp
from jax import lax
from jax.experimental import pallas as pl
from jax.experimental.pallas import tpu as pltpu
from jax.sharding import PartitionSpec as P

SIDE = 7
PIX = 49
MICRO = 2
PIECES = 16
EPSILON = 1e-05
HIGH = lax.Precision.HIGHEST
BF = jnp.bfloat16
F32 = jnp.float32
MESH = pl.DeviceIdType.MESH
LANES = 128
HALF = 256
ROW = 512
GRID = SIDE + 2
WEIGHTS = ("red", "spa", "exp", "squ", "mot", "con", "gat")
SMALL = ("squ", "mot", "con", "gat")
CHUNKS = ("a", "b", "c")
COMPS = ("red", "spa", "exp", "small")
HOLDS = dict(a=("exp", "small"), b=("spa",), c=("red",))


def sigmoid(values):
    return 0.5 * jnp.tanh(0.5 * values) + 0.5


def silu_slope(values):
    sigma = sigmoid(values)
    return sigma * (1.0 + values * (1.0 - sigma))


def dot(a, b):
    return jnp.dot(a, b, preferred_element_type=F32)


def dot_nt(a, b):
    return lax.dot_general(a, b, (((1,), (1,)), ((), ())), preferred_element_type=F32)


def dot_tn(a, b):
    return lax.dot_general(a, b, (((0,), (0,)), ((), ())), preferred_element_type=F32)


def up(value, step):
    return -(-value // step) * step


def plan(n, ch, mid, red, segs, share):
    side = 4 if n % 64 == 0 else 2 if n % 4 == 0 else 1
    depth = n // (side * side)
    slots = PIECES // (side * side)
    levels = [(n, 1)] if n <= 16 else [(side * side, 1), (depth, side * side)]
    rows = dict(red=ch * mid // ROW, spa=9 * mid * mid // ROW, exp=mid * ch // ROW)
    small = mid * red + 9 * red * red + red * red + red * mid + mid
    small_rows = up(small, ROW) // ROW
    parts = dict(
        red=(0, rows["red"] // PIECES),
        spa=(rows["red"], rows["spa"] // PIECES),
        exp=(rows["red"] + rows["spa"], rows["exp"] // PIECES),
        small=(rows["red"] + rows["spa"] + rows["exp"], up(up(small_rows, PIECES) // PIECES, 16)),
    )
    total = (parts["small"][0] + small_rows) * ROW
    margin = max(size for _, size in parts.values())
    reach = 1
    for start, size in parts.values():
        for piece in range(PIECES):
            first = (start + size * piece) * ROW
            if first < total:
                last = min((start + size * (piece + 1)) * ROW, total) - 1
                reach = max(reach, last // share - first // share + 1)
    land = margin + up(share // ROW + 18, 16) + margin
    return SimpleNamespace(
        side=side,
        depth=depth,
        slots=slots,
        levels=levels,
        parts=parts,
        total=total,
        margin=margin,
        reach=reach,
        land=land,
        small_rows=small_rows,
    )


def kernel(n, sizes, names, *refs):
    r = SimpleNamespace(**dict(zip(names, refs)))
    own_w = dict(
        red=r.in_red, spa=r.in_spa, exp=r.in_exp, squ=r.in_squ, mot=r.in_mot, con=r.in_con, gat=r.in_gat
    )
    sib_w = dict(
        red=r.sib_red, spa=r.sib_spa, exp=r.sib_exp, squ=r.sib_squ, mot=r.sib_mot, con=r.sib_con, gat=r.sib_gat
    )
    held_w = dict(red=r.red, spa=r.spa, exp=r.exp, squ=r.squ, mot=r.mot, con=r.con, gat=r.gat)
    chunk_refs = dict(
        a=SimpleNamespace(g=r.g_a, r0=r.r0_a, r1=r.r1_a, r2=r.r2_a, r3=r.r3_a),
        b=SimpleNamespace(g=r.g_b, r0=r.r0_b, r1=r.r1_b, r2=r.r2_b, r3=r.r3_b),
        c=SimpleNamespace(g=r.g_c, r0=r.r0_c, r1=r.r1_c, r2=r.r2_c, r3=r.r3_c),
    )
    fin = dict(red=r.fin_red, spa=r.fin_spa, exp=r.fin_exp, small=r.fin_small)
    ch, mid, red_w, segs, share = sizes
    pp = plan(n, ch, mid, red_w, segs, share)
    side, depth, slots, levels, parts = pp.side, pp.depth, pp.slots, pp.levels, pp.parts
    rows = PIX * segs
    full = up(rows, 16)
    pad = full - rows
    c = lax.axis_index("pipe")
    i = lax.axis_index("dp")
    x = lax.rem(i, side)
    y = lax.rem(lax.div(i, side), side)
    z = lax.div(i, side * side)
    fc = x * (1 - c) + y * c
    gc = y * (1 - c) + x * c
    other = (1 - c, i)

    def remote(src, dst, send, recv, device):
        return pltpu.make_async_remote_copy(
            src_ref=src,
            dst_ref=dst,
            send_sem=send,
            recv_sem=recv,
            device_id=device,
            device_id_type=MESH,
        )

    barrier = pltpu.get_barrier_semaphore()

    def greet(k, _):
        peer = lax.rem(i + k, n)
        pl.semaphore_signal(barrier, inc=1, device_id=(c, peer), device_id_type=MESH)
        pl.semaphore_signal(barrier, inc=1, device_id=(1 - c, peer), device_id_type=MESH)
        return 0

    pl.semaphore_signal(barrier, inc=1, device_id=other, device_id_type=MESH)
    lax.fori_loop(1, n, greet, 0)

    count_own = r.counts[c]
    segment = lax.broadcasted_iota(jnp.int32, (segs, LANES), 0)
    valid = jnp.where(segment < count_own, 1.0, 0.0).astype(F32)
    paired = jnp.where(segment + 1 < count_own, 1.0, 0.0).astype(F32)
    pixels_own = PIX * count_own.astype(F32)

    stage = r.stage
    v = r.v
    free = r.nh3.at[1]

    def tile(j):
        return pl.ds(pl.multiple_of(j * LANES, LANES), LANES)

    def view(j, base=0):
        return (
            pl.ds(pl.multiple_of(base + lax.div(j, 4) * full, 16), rows),
            tile(lax.rem(j, 4)),
        )

    def loop(count, body):
        def step(j, _):
            body(j)
            return 0

        lax.fori_loop(0, count, step, 0)

    def packed(values):
        flat = values.reshape(rows, values.shape[-1])
        return jnp.concatenate([flat, jnp.zeros((pad, flat.shape[-1]), F32)], axis=0).astype(BF)

    def cube(values):
        return values.reshape(PIX, segs, values.shape[-1])

    def fold(values):
        return jnp.sum(jnp.sum(values, axis=0), axis=0, keepdims=True)

    load_frames = pltpu.make_async_copy(r.frames.at[c], stage.at[0], r.load_sem.at[0])
    load_frames.start()

    def load_weight(name, s, first):
        @pl.when(c == s)
        def _():
            pltpu.make_async_copy(own_w[name], held_w[name], r.w_sem.at[WEIGHTS.index(name)]).start()

        @pl.when(c != s)
        def _():
            if first:
                k = WEIGHTS.index(name)
                remote(
                    own_w[name], sib_w[name], r.ws_sem.at[k], r.wr_sem.at[k], other
                ).wait_recv()
            pltpu.make_async_copy(
                sib_w[name], held_w[name], r.w_sem.at[WEIGHTS.index(name)]
            ).start()

    def wait_weight(name):
        pltpu.make_async_copy(own_w[name], held_w[name], r.w_sem.at[WEIGHTS.index(name)]).wait()

    own_params = [
        pltpu.make_async_copy(r.in_norm, r.norm.at[c], r.p_sem.at[0]),
        pltpu.make_async_copy(r.in_bias, r.bias.at[c], r.p_sem.at[1]),
    ]
    for copy in own_params:
        copy.start()

    r.grid[...] = jnp.zeros(r.grid.shape, F32)

    pl.semaphore_wait(barrier, 2 * n - 1)

    weight_sends = []
    for k, name in enumerate(WEIGHTS):
        copy = remote(
            own_w[name], sib_w[name], r.ws_sem.at[k], r.wr_sem.at[k], other
        )
        copy.start()
        weight_sends.append(copy)
    param_sends = [
        remote(r.in_norm, r.norm.at[c], r.ps_sem.at[0], r.pr_sem.at[0], other),
        remote(r.in_bias, r.bias.at[c], r.ps_sem.at[1], r.pr_sem.at[1], other),
    ]
    for copy in param_sends:
        copy.start()

    msg, inbox = r.msg, r.inbox
    exchanges = [0]

    def peer_of(level, k):
        size, stride = levels[level]
        here = lax.rem(lax.div(i, stride), size)
        return (c, i + (lax.rem(here + k, size) - here) * stride)

    def copies_of(par, level, size_rows):
        size, _ = levels[level]
        return [
            remote(
                msg.at[par, level, pl.ds(0, size_rows)],
                inbox.at[par, level, k, pl.ds(0, size_rows)],
                r.ms_sem.at[par, level, k],
                r.mr_sem.at[par, level, k],
                peer_of(level, k),
            )
            for k in range(1, size)
        ]

    def exchange_start(size_rows):
        par = exchanges[0] % 2
        exchanges[0] += 1
        copies = copies_of(par, 0, size_rows)
        for copy in copies:
            copy.start()
        return (par, size_rows, copies)

    def exchange_finish(handle, combine):
        par, size_rows, copies = handle
        for level in range(len(levels)):
            if level:
                copies = copies_of(par, level, size_rows)
                for copy in copies:
                    copy.start()
            for copy in copies:
                copy.wait_recv()
            result = combine(par, level)
            for copy in copies:
                copy.wait_send()
            if level + 1 < len(levels):
                msg[par, level + 1, 0:size_rows, :] = result
        return result

    cnt = r.cnt

    def count_copies(level):
        size, _ = levels[level]
        return [
            remote(
                cnt.at[level, 0],
                cnt.at[level, k],
                r.cs_sem.at[level, k],
                r.cr_sem.at[level, k],
                peer_of(level, k),
            )
            for k in range(1, size)
        ]

    cnt[0, 0] = jnp.full((8, LANES), pixels_own, F32)
    for copy in count_copies(0):
        copy.start()

    def count_finish():
        for level in range(len(levels)):
            copies = count_copies(level)
            if level:
                for copy in copies:
                    copy.start()
            total = cnt[level, 0]
            for k, copy in enumerate(copies):
                copy.wait()
                total = total + cnt[level, k + 1]
            if level + 1 < len(levels):
                cnt[level + 1, 0] = total
        r.total[...] = total

    def sum_combine(nt):
        def combine(par, level):
            size, _ = levels[level]
            total = msg[par, level, 0 : 2 * nt, :]
            for k in range(1, size):
                total = total + inbox[par, level, k, 0 : 2 * nt, :]
            return total

        return combine

    def moment_combine(nt):
        def combine(par, level):
            size, _ = levels[level]

            def slot(k):
                if k == 0:
                    return msg[par, level, 0 : 2 * nt, :]
                return inbox[par, level, k, 0 : 2 * nt, :]

            items = [slot(k) for k in range(size)]
            counts = [r.cnt[level, k, 0:1, :] for k in range(size)]
            total = items[0][0:nt]
            count = counts[0]
            for k in range(1, size):
                total = total + items[k][0:nt]
                count = count + counts[k]
            mean = total / count
            spread = jnp.zeros_like(total)
            for k in range(size):
                gap = items[k][0:nt] / counts[k] - mean
                spread = spread + items[k][nt : 2 * nt] + counts[k] * gap * gap
            return jnp.concatenate([total, spread], axis=0)

        return combine

    def norm_send(ref, nt):
        par = exchanges[0] % 2

        def body(j):
            values = cube(ref[view(j)])
            total = fold(values * valid)
            gap = (values - total / pixels_own) * valid
            msg[par, 0, pl.ds(j, 1), :] = total
            msg[par, 0, pl.ds(nt + j, 1), :] = fold(gap * gap)

        loop(nt, body)
        return exchange_start(2 * nt)

    def norm_receive(handle, nt, s, row0):
        result = exchange_finish(handle, moment_combine(nt))
        everyone = r.total[0:1, :]
        r.mean[0:nt, :] = result[0:nt] / everyone
        r.rstd[s, row0 : row0 + nt, :] = lax.rsqrt(result[nt : 2 * nt] / everyone + EPSILON)

    def gain_of(s, offset, j):
        lanes = pl.ds(pl.multiple_of(offset + j * LANES, LANES), LANES)
        return (r.norm[s, 0:1, lanes], r.norm[s, 1:2, lanes])

    def row_of(ref, j):
        return ref[pl.ds(j, 1), :]

    grid = r.grid

    def to_grid(values, lanes):
        for h in range(SIDE):
            at = ((h + 1) * GRID + 1) * segs
            grid[at : at + SIDE * segs, lanes] = values[h * SIDE * segs : (h + 1) * SIDE * segs]

    def patches(target, width, flip):
        def body(j):
            lanes = tile(j)
            for tap in range(9):
                down, right = tap // 3, tap % 3
                if flip:
                    down, right = 2 - down, 2 - right
                pieces = []
                for h in range(SIDE):
                    at = ((h + down) * GRID + right) * segs
                    pieces.append(grid[at : at + SIDE * segs, lanes])
                target[:, pl.ds(pl.multiple_of(tap * width + j * LANES, LANES), LANES)] = packed(
                    jnp.concatenate(pieces, axis=0)
                )

        loop(width // LANES, body)

    def put(slot, target, kind, s):
        @pl.when(c == s)
        def _():
            pltpu.make_async_copy(stage.at[slot], target.at[c], r.o_sem.at[kind, 0]).start()

        @pl.when(c != s)
        def _():
            remote(
                stage.at[slot],
                target.at[c],
                r.o_sem.at[kind, 1],
                r.o_sem.at[kind, 2],
                other,
            ).start()

    def put_wait(slot, target, kind, s):
        @pl.when(c == s)
        def _():
            pltpu.make_async_copy(stage.at[slot], target.at[c], r.o_sem.at[kind, 0]).wait()

        @pl.when(c != s)
        def _():
            remote(
                stage.at[slot],
                target.at[c],
                r.o_sem.at[kind, 1],
                r.o_sem.at[kind, 2],
                other,
            ).wait_send()

    def stage_to_v(slot):
        def body(j):
            v[:, tile(j)] = packed(stage[slot, :, :, tile(j)].astype(F32))

        loop(ch // LANES, body)

    n_mid = mid // LANES
    n_ch = ch // LANES

    for name in WEIGHTS:
        load_weight(name, 0, True)
    load_frames.wait()
    stage_to_v(0)
    for copy in own_params:
        copy.wait()
    for copy in param_sends:
        copy.wait_recv()

    for s in range(2):
        nh1, nh2, nh3 = r.nh1.at[s], r.nh2.at[s], r.nh3.at[s]
        wait_weight("red")
        nh1[...] = dot(v[...], r.red[...])
        if s == 0:
            load_weight("red", 1, True)
        handle = norm_send(nh1, n_mid)
        if s == 0:
            count_finish()
        norm_receive(handle, n_mid, s, 0)

        def act_one(j, s=s, nh1=nh1):
            gain, offset = gain_of(s, 0, j)
            normed = (nh1[view(j)] - row_of(r.mean, j)) * row_of(r.rstd.at[s], j)
            nh1[view(j)] = normed
            before = normed * gain + offset
            act = before * sigmoid(before)
            r.a1[s, :, tile(j)] = packed(act)
            to_grid(act, tile(j))

        loop(n_mid, act_one)
        patches(r.patch, mid, False)
        wait_weight("spa")
        nh2[...] = dot(r.patch[...], r.spa[...])
        if s == 0:
            load_weight("spa", 1, True)
        handle = norm_send(nh2, n_mid)
        norm_receive(handle, n_mid, s, n_mid)

        def act_two(j, s=s, nh2=nh2):
            gain, offset = gain_of(s, mid, j)
            normed = (nh2[view(j)] - row_of(r.mean, j)) * row_of(r.rstd.at[s], n_mid + j)
            nh2[view(j)] = normed
            before = normed * gain + offset
            r.h2[s, :, tile(j)] = packed(before * sigmoid(before))

        loop(n_mid, act_two)
        for name in SMALL:
            wait_weight(name)
        squeezed = cube(dot(r.h2[s], r.squ[...])[:rows])
        later = pltpu.roll(squeezed, segs - 1, 1)
        field = (paired * (later - squeezed)).reshape(rows, red_w)
        r.field[s] = packed(field)
        rounded = r.field[s].astype(F32)[:rows]
        to_grid(rounded, pl.ds(0, LANES))
        patches(r.patch_m, red_w, False)
        context_mean = jnp.sum(cube(rounded), axis=0) * (1.0 / PIX)
        r.cmean[s] = context_mean
        from_mean = jnp.dot(
            context_mean, r.con[...].astype(F32), precision=HIGH, preferred_element_type=F32
        )
        mixed = cube(dot(r.patch_m[...], r.mot[...])[:rows]) + from_mean
        r.score[s] = packed(mixed)
        free[0:full, :] = dot(r.score[s], r.gat[...])

        def gate(j, s=s):
            bias = r.bias[s, 0:1, tile(j)]
            sigma = sigmoid(free[view(j)] + bias)
            r.sigma[s, 0:rows, tile(j)] = sigma
            h2 = r.h2[s, :, tile(j)].astype(F32)[:rows]
            r.gated[s, :, tile(j)] = packed(h2 * (0.5 + sigma))

        loop(n_mid, gate)
        if s == 0:
            for name in SMALL:
                load_weight(name, 1, True)
        wait_weight("exp")
        for block in range(ch // ROW):
            nh3[block * full : (block + 1) * full, :] = dot(
                r.gated[s], r.exp[:, block * ROW : (block + 1) * ROW]
            )
        if s == 0:
            load_weight("exp", 1, True)
        handle = norm_send(nh3, n_ch)
        norm_receive(handle, n_ch, s, 2 * n_mid)
        slot = 1 - s

        def finish(j, s=s, nh3=nh3, slot=slot):
            gain, offset = gain_of(s, 2 * mid, j)
            normed = (nh3[view(j)] - row_of(r.mean, j)) * row_of(
                r.rstd.at[s], 2 * n_mid + j
            )
            nh3[view(j)] = normed
            before = v[:, tile(j)].astype(F32)[:rows] + normed * gain + offset
            out = cube(before * sigmoid(before)) * valid
            stage[slot, :, :, tile(j)] = out.astype(BF)
            if s == 0:
                v[:, tile(j)] = packed(out)

        loop(n_ch, finish)
        put(slot, r.out, s, s)
        if s == 0:
            put_wait(slot, r.out, 0, 0)
            load_grad = pltpu.make_async_copy(r.out_grad.at[c], stage.at[1], r.load_sem.at[1])
            load_grad.start()

    def send_sem(chunk, k):
        return r.rs_send.at[CHUNKS.index(chunk), k]

    def recv_sem(chunk, k):
        return r.rs_recv.at[CHUNKS.index(chunk), k]

    def add_loop(target, others, pieces):
        def body(j):
            at = target.at[j]
            total = at[...]
            for item in others:
                total = total + item.at[j][...]
            at[...] = total

        loop(pieces, body)

    def rs0(chunk):
        return [
            remote(
                chunk_refs[chunk].g.at[1 - c],
                chunk_refs[chunk].r0,
                send_sem(chunk, 0),
                recv_sem(chunk, 0),
                other,
            )
        ]

    def device_at(f, g, depth_at):
        px = f * (1 - c) + g * c
        py = g * (1 - c) + f * c
        return (c, depth_at * side * side + py * side + px)

    def rs1(chunk):
        found = []
        for k in range(1, side):
            f = lax.rem(fc + k, side)
            found.append(
                remote(
                    chunk_refs[chunk].g.at[c, f],
                    chunk_refs[chunk].r1.at[k - 1],
                    send_sem(chunk, k),
                    recv_sem(chunk, k),
                    device_at(f, gc, z),
                )
            )
        return found

    def rs2(chunk):
        found = []
        for k in range(1, side):
            g = lax.rem(gc + k, side)
            found.append(
                remote(
                    chunk_refs[chunk].g.at[c, fc, g],
                    chunk_refs[chunk].r2.at[k - 1],
                    send_sem(chunk, side - 1 + k),
                    recv_sem(chunk, side - 1 + k),
                    device_at(fc, g, z),
                )
            )
        return found

    def rs3(chunk):
        found = []
        for k in range(1, depth):
            to = lax.rem(z + k, depth)
            copy = remote(
                chunk_refs[chunk].g.at[c, fc, gc, lax.rem(to, slots)],
                chunk_refs[chunk].r3.at[k - 1],
                send_sem(chunk, 2 * (side - 1) + k),
                recv_sem(chunk, 2 * (side - 1) + k),
                device_at(fc, gc, to),
            )
            found.append((to, copy))
        return found

    def go(copies):
        for copy in copies:
            copy.start()

    def rs0_start(chunk):
        go(rs0(chunk))

    def rs1_start(chunk):
        for copy in rs0(chunk):
            copy.wait()
        own = chunk_refs[chunk].g.at[c]
        r0 = chunk_refs[chunk].r0
        for f in range(side):
            for g in range(side):
                add_loop(own.at[f, g], [r0.at[f, g]], slots)
        go(rs1(chunk))

    def rs2_start(chunk):
        copies = rs1(chunk)
        for copy in copies:
            copy.wait_recv()
        own = chunk_refs[chunk].g.at[c, fc]
        r1 = chunk_refs[chunk].r1
        for g in range(side):
            add_loop(own.at[g], [r1.at[k, g] for k in range(side - 1)], slots)
        for copy in copies:
            copy.wait_send()
        go(rs2(chunk))

    def rs3_start(chunk):
        copies = rs2(chunk)
        for copy in copies:
            copy.wait_recv()
        r2 = chunk_refs[chunk].r2
        add_loop(chunk_refs[chunk].g.at[c, fc, gc], [r2.at[k] for k in range(side - 1)], slots)
        for copy in copies:
            copy.wait_send()
        for to, copy in rs3(chunk):
            if slots == depth:
                copy.start()
            else:
                pl.when(to < slots)(copy.start)

    def owners(comp):
        start, size = parts[comp]
        at = start + size * i
        first = lax.div(at * ROW, share)
        last = lax.div(jnp.minimum((at + size) * ROW, pp.total) - 1, share)
        exists = jnp.logical_and(i < PIECES, at * ROW < pp.total)
        return at, first, last, exists

    def send_piece(comp, s, action):
        _, size = parts[comp]
        at, first, last, exists = owners(comp)
        which = COMPS.index(comp)
        for k in range(pp.reach):
            to = first + k
            base = lax.div(to * share, ROW * 16) * 16
            row = pl.multiple_of(pp.margin + at - base, 16)
            there = r.land.at[pl.ds(row, size), pl.ds(pl.multiple_of(c * HALF, HALF), HALF)]
            needed = jnp.logical_and(exists, to <= last)
            here = jnp.logical_and(c == s, to == i)
            source = fin[comp]
            arrival = r.land_sem.at[which, c, lax.rem(i, PIECES)]

            @pl.when(jnp.logical_and(needed, here))
            def _():
                copy = pltpu.make_async_copy(source, there, arrival)
                if action == "start":
                    copy.start()
                else:
                    copy.wait()

            @pl.when(jnp.logical_and(needed, jnp.logical_not(here)))
            def _():
                copy = remote(source, there, r.fin_sem.at[which, k], arrival, (s, to))
                if action == "start":
                    copy.start()
                else:
                    copy.wait_send()

    def finish_chunk(chunk, s):
        own = chunk_refs[chunk].g.at[c, fc, gc]
        r3 = chunk_refs[chunk].r3
        copies = rs3(chunk)

        def work():
            for _, copy in copies:
                copy.wait_recv()
            mine = own.at[lax.rem(z, slots)]

            def summed(first, count):
                total = mine[first : first + count, :].astype(F32)
                for k in range(depth - 1):
                    total = total + r3[k, first : first + count, :].astype(F32)
                return total

            mix = r.mix

            def weave(first, count, stride, value):
                for k in range(HALF // LANES):
                    mix[k, pl.ds(first, count, stride=stride), :] = value[
                        :, k * LANES : (k + 1) * LANES
                    ]

            def woven(target, size):
                for k in range(HALF // LANES):
                    target[:, k * LANES : (k + 1) * LANES] = mix[k, 0:size, :].astype(BF)

            cins = mid // PIECES
            if chunk == "a":
                size = parts["exp"][1]
                quarters = size // cins
                for q in range(quarters):
                    weave(q, cins, quarters, summed(q * cins, cins))
                woven(r.fin_exp, size)
                r.fin_small[...] = summed(size, parts["small"][1]).astype(BF)
            elif chunk == "b":
                size = parts["spa"][1]
                for tap in range(9):
                    weave(tap, cins, 9, summed(tap * cins, cins))
                woven(r.fin_spa, size)
            else:
                r.fin_red[...] = summed(0, parts["red"][1]).astype(BF)

        if slots == depth:
            work()
        else:
            pl.when(z < slots)(work)
        for to, copy in copies:
            if slots == depth:
                copy.wait_send()
            else:
                pl.when(to < slots)(copy.wait_send)
        for comp in HOLDS[chunk]:
            send_piece(comp, s, "start")

    def finish_sent(chunk, s):
        for comp in HOLDS[chunk]:
            send_piece(comp, s, "wait")

    def place(half, piece):
        px, py, pz = piece % side, (piece // side) % side, piece // (side * side)
        return (half, px, py, pz) if half == 0 else (half, py, px, pz)

    small_at = 2 * full

    def grads_a(s):
        cins = mid // PIECES
        g = r.g_a
        for q in range(ch // ROW):
            for half in range(2):
                lanes = slice(q * ROW + half * HALF, q * ROW + (half + 1) * HALF)
                value = dot_tn(r.gated[s], r.gz3[:, lanes]).astype(BF)
                for piece in range(PIECES):
                    where = place(half, piece)
                    g[where + (slice(q * cins, (q + 1) * cins),)] = value[
                        piece * cins : (piece + 1) * cins
                    ]
        tmp = r.tmp1
        at = small_at
        per = ROW // LANES

        def spread(count):
            for q in range(per):
                free[at : at + count, q * LANES : (q + 1) * LANES] = tmp[
                    pl.ds(q, count, stride=per), :
                ]

        tmp[0:mid, :] = dot_tn(r.h2[s], r.gr[...])
        spread(mid // per)
        at += mid // per
        moved = dot_tn(r.field[s], r.patch_m[...])
        for tap in range(9):
            tmp[pl.ds(tap, red_w, stride=9), :] = moved[:, tap * LANES : (tap + 1) * LANES]
        spread(9 * red_w // per)
        at += 9 * red_w // per
        tmp[0:red_w, :] = lax.dot_general(
            r.cmean[s],
            r.ssum[...],
            (((0,), (0,)), ((), ())),
            precision=HIGH,
            preferred_element_type=F32,
        )
        spread(red_w // per)
        at += red_w // per
        free[at : at + red_w, :] = dot_tn(r.score[s], r.gl[...])
        at += red_w
        free[at : at + 8, :] = jnp.broadcast_to(r.gbias[...], (8, mid))
        start = parts["exp"][1]
        size = parts["small"][1]
        used = -(-pp.small_rows // size)
        for piece in range(PIECES):
            for half in range(2):
                where = place(half, piece) + (slice(start, start + size),)
                if piece < used:
                    g[where] = free[
                        small_at + piece * size : small_at + (piece + 1) * size,
                        half * HALF : (half + 1) * HALF,
                    ].astype(BF)
                else:
                    g[where] = jnp.zeros((size, HALF), BF)

    def grads_b(s):
        cins = mid // PIECES
        g = r.g_b

        def body(tap):
            for half in range(2):
                lanes = pl.ds(pl.multiple_of(tap * mid + half * HALF, HALF), HALF)
                value = dot_tn(r.a1[s], r.patch[:, lanes]).astype(BF)
                for piece in range(PIECES):
                    where = place(half, piece)
                    g[where + (pl.ds(pl.multiple_of(tap * cins, cins), cins),)] = value[
                        piece * cins : (piece + 1) * cins
                    ]

        loop(9, body)

    def grads_c(s):
        g = r.g_c
        size = parts["red"][1]
        for half in range(2):
            value = dot_tn(v[...], r.gz1[:, half * HALF : (half + 1) * HALF]).astype(BF)
            for piece in range(PIECES):
                g[place(half, piece)] = value[piece * size : (piece + 1) * size]

    def back_receive(handle, nt, s, row0):
        result = exchange_finish(handle, sum_combine(nt))
        half_rows = 2 * n_mid + n_ch
        r.gnorm[s, row0 : row0 + nt, :] = result[nt : 2 * nt]
        r.gnorm[s, half_rows + row0 : half_rows + row0 + nt, :] = result[0:nt]
        r.bsum[0 : 2 * nt, :] = result / r.total[0:1, :]

    def norm_grad(grad, normed, s, offset, row0, nt, j):
        gain, _ = gain_of(s, offset, j)
        scale = gain * row_of(r.rstd.at[s], row0 + j)
        mean_grad = row_of(r.bsum, j)
        mean_cross = row_of(r.bsum, nt + j)
        return scale * (cube(grad) - valid * (mean_grad + cube(normed) * mean_cross))

    def slope_send(s, grad_at, normed_ref, offset, nt):
        par = exchanges[0] % 2

        def body(j):
            gain, shift = gain_of(s, offset, j)
            normed = normed_ref[view(j)]
            grad = free[view(j, grad_at)] * silu_slope(normed * gain + shift)
            free[view(j, grad_at)] = grad
            msg[par, 0, pl.ds(j, 1), :] = fold(cube(grad))
            msg[par, 0, pl.ds(nt + j, 1), :] = fold(cube(grad * normed))

        loop(nt, body)
        return exchange_start(2 * nt)

    gs = r.gs
    for s in (1, 0):
        nh1, nh2, nh3 = r.nh1.at[s], r.nh2.at[s], r.nh3.at[s]
        slot = s
        if s == 1:
            load_grad.wait()
        par = exchanges[0] % 2

        def back_three(j, s=s, nh3=nh3, slot=slot, par=par):
            gain, shift = gain_of(s, 2 * mid, j)
            normed = nh3[view(j)]
            before = v[:, tile(j)].astype(F32)[:rows] + normed * gain + shift
            grad = cube(silu_slope(before)) * valid * stage[slot, :, :, tile(j)].astype(F32)
            gs[view(j)] = grad.reshape(rows, LANES)
            msg[par, 0, pl.ds(j, 1), :] = fold(grad)
            msg[par, 0, pl.ds(n_ch + j, 1), :] = fold(grad * cube(normed))

        loop(n_ch, back_three)
        handle = exchange_start(2 * n_ch)
        if s == 0:
            rs1_start("c")
            rs3_start("a")
        back_receive(handle, n_ch, s, 2 * n_mid)

        def grad_three(j, s=s, nh3=nh3):
            r.gz3[:, tile(j)] = packed(
                norm_grad(gs[view(j)], nh3[view(j)], s, 2 * mid, 2 * n_mid, n_ch, j)
            )

        loop(n_ch, grad_three)
        if s == 0:
            wait_weight("exp")
        free[0:full, :] = dot_nt(r.gz3[...], r.exp[...])
        if s == 1:
            load_weight("exp", 0, False)

        def back_gate(j, s=s):
            grad = free[view(j)]
            sigma = r.sigma[s, 0:rows, tile(j)]
            h2 = r.h2[s, :, tile(j)].astype(F32)[:rows]
            free[view(j, full)] = grad * (0.5 + sigma)
            value = packed(grad * h2 * sigma * (1.0 - sigma))
            r.gl[:, tile(j)] = value
            r.gbias[0:1, tile(j)] = fold(cube(value.astype(F32)[:rows]))

        loop(n_mid, back_gate)
        if s == 0:
            for name in SMALL:
                wait_weight(name)
        r.gq[...] = dot_nt(r.gl[...], r.gat[...]).astype(BF)
        rounded = r.gq[...].astype(F32)[:rows]
        to_grid(rounded, pl.ds(0, LANES))
        patches(r.patch_m, red_w, True)
        score_sums = jnp.sum(cube(rounded), axis=0)
        r.ssum[...] = score_sums
        grad_field = None
        for tap in range(9):
            part = dot_nt(
                r.patch_m[:, tap * red_w : (tap + 1) * red_w],
                r.mot[tap * red_w : (tap + 1) * red_w, :],
            )
            grad_field = part if grad_field is None else grad_field + part
        from_mean = lax.dot_general(
            score_sums,
            r.con[...].astype(F32),
            (((1,), (1,)), ((), ())),
            precision=HIGH,
            preferred_element_type=F32,
        ) * (1.0 / PIX)
        weighted = paired * (cube(grad_field[:rows]) + from_mean)
        r.gr[...] = packed(pltpu.roll(weighted, 1, 1) - weighted)
        free[full : 2 * full, :] += dot_nt(r.gr[...], r.squ[...])
        if s == 1:
            for name in SMALL:
                load_weight(name, 0, False)
        handle = slope_send(s, full, nh2, mid, n_mid)
        if s == 0:
            finish_chunk("a", 1)
            rs3_start("b")
        grads_a(s)
        rs0_start("a")
        back_receive(handle, n_mid, s, n_mid)

        def grad_two(j, s=s, nh2=nh2):
            value = norm_grad(free[view(j, full)], nh2[view(j)], s, mid, n_mid, n_mid, j)
            to_grid(value.reshape(rows, LANES), tile(j))

        loop(n_mid, grad_two)
        patches(r.patch, mid, True)
        if s == 0:
            wait_weight("spa")
        acc = None
        for tap in range(9):
            part = dot_nt(
                r.patch[:, tap * mid : (tap + 1) * mid], r.spa[tap * mid : (tap + 1) * mid, :]
            )
            acc = part if acc is None else acc + part
        free[0:full, :] = acc
        if s == 1:
            load_weight("spa", 0, False)
        handle = slope_send(s, 0, nh1, 0, n_mid)
        if s == 0:
            finish_chunk("b", 1)
            rs2_start("c")
        grads_b(s)
        rs0_start("b")
        rs1_start("a")
        back_receive(handle, n_mid, s, 0)

        def grad_one(j, s=s, nh1=nh1):
            r.gz1[:, tile(j)] = packed(
                norm_grad(free[view(j)], nh1[view(j)], s, 0, 0, n_mid, j)
            )

        loop(n_mid, grad_one)
        if s == 0:
            rs3_start("c")
            finish_chunk("c", 1)
        rs1_start("b")
        grads_c(s)
        rs0_start("c")
        rs2_start("a")
        if s == 1:
            put_wait(0, r.out, 1, 1)
            reload = pltpu.make_async_copy(r.frames.at[c], stage.at[1], r.load_sem.at[0])
            reload.start()
        else:
            wait_weight("red")
        slot = 1 - s
        for block in range(ch // ROW):
            value = gs[block * full : block * full + rows, :] + dot_nt(
                r.gz1[...], r.red[block * ROW : (block + 1) * ROW, :]
            )[:rows]
            stage[slot, :, :, block * ROW : (block + 1) * ROW] = cube(value).astype(BF)
        put(slot, r.ing, 2 + s, s)
        if s == 1:
            load_weight("red", 0, False)
            rs2_start("b")
            reload.wait()
            stage_to_v(1)

    gn_send = remote(
        r.gnorm.at[1 - c], r.gnorm_in, r.gn_sem.at[0], r.gn_sem.at[1], other
    )
    gn_send.start()
    for chunk in CHUNKS:
        finish_sent(chunk, 1)
    rs1_start("c")
    rs3_start("a")
    rs2_start("b")
    rs2_start("c")
    finish_chunk("a", 0)
    rs3_start("b")
    rs3_start("c")
    finish_chunk("b", 0)
    finish_chunk("c", 0)
    gn_send.wait()
    r.gnorm_out[...] = r.gnorm[c] + r.gnorm_in[...]

    for copy in weight_sends + param_sends:
        copy.wait_send()
    put_wait(0, r.ing, 3, 1)
    put_wait(1, r.ing, 2, 0)
    for base, target in ((0, r.out), (2, r.ing)):
        for s in range(2):

            @pl.when(c == s)
            def _():
                remote(
                    stage.at[0],
                    target.at[1 - c],
                    r.o_sem.at[base + s, 1],
                    r.o_sem.at[base + s, 2],
                    other,
                ).wait_recv()

    for chunk in CHUNKS:
        finish_sent(chunk, 0)
    low = i * share
    high = low + share
    for which, comp in enumerate(COMPS):
        start, size = parts[comp]

        def arrive(piece, _):
            first = (start + size * piece) * ROW
            last = jnp.minimum(first + size * ROW, pp.total)

            @pl.when(jnp.logical_and(first < high, last > low))
            def _():
                for core in range(2):
                    own = jnp.logical_and(c == core, i == piece)

                    @pl.when(jnp.logical_not(own))
                    def _():
                        pltpu.make_async_copy(
                            fin[comp],
                            r.land.at[pl.ds(0, size), pl.ds(0, HALF)],
                            r.land_sem.at[which, core, piece],
                        ).wait()

            return 0

        lax.fori_loop(0, PIECES, arrive, 0)


def run(n, sizes, frames, out_grad, seg_counts, weights, bias, norm):
    ch, mid, red_w, segs, share = sizes
    pp = plan(n, ch, mid, red_w, segs, share)
    side, depth, slots, levels, parts = pp.side, pp.depth, pp.slots, pp.levels, pp.parts
    rows = PIX * segs
    full = up(rows, 16)
    norm_rows = 2 * (2 * mid + ch) // LANES
    group = max(size for size, _ in levels)
    any_spec = pl.BlockSpec(memory_space=pl.ANY)
    vmem_spec = pl.BlockSpec(memory_space=pltpu.VMEM)

    ins = dict(
        frames=frames,
        out_grad=out_grad,
        in_red=weights.red,
        in_spa=weights.spa,
        in_exp=weights.exp,
        in_squ=weights.squ,
        in_mot=weights.mot,
        in_con=weights.con,
        in_gat=weights.gat,
        counts=seg_counts,
        in_bias=bias,
        in_norm=norm,
    )
    in_specs = [any_spec] * 9 + [pl.BlockSpec(memory_space=pltpu.SMEM), vmem_spec, vmem_spec]

    def like(item):
        return jax.ShapeDtypeStruct(item.shape, item.dtype)

    outs = dict(
        out=like(frames),
        ing=like(frames),
        land=jax.ShapeDtypeStruct((pp.land, ROW), BF),
        sib_red=like(weights.red),
        sib_spa=like(weights.spa),
        sib_exp=like(weights.exp),
        sib_squ=like(weights.squ),
        sib_mot=like(weights.mot),
        sib_con=like(weights.con),
        sib_gat=like(weights.gat),
        gnorm_out=jax.ShapeDtypeStruct((norm_rows, LANES), F32),
    )
    out_specs = [any_spec] * 10 + [vmem_spec]

    def low(*dims):
        return pltpu.VMEM(dims, BF)

    def wide(*dims):
        return pltpu.VMEM(dims, F32)

    def sems(*dims):
        return pltpu.SemaphoreType.DMA(dims)

    def piled(size):
        return (
            low(2, side, side, slots, size, HALF),
            low(side, side, slots, size, HALF),
            low(max(side - 1, 1), side, slots, size, HALF),
            low(max(side - 1, 1), slots, size, HALF),
            low(max(depth - 1, 1), size, HALF),
        )

    pile_a = piled(parts["exp"][1] + parts["small"][1])
    pile_b = piled(parts["spa"][1])
    pile_c = piled(parts["red"][1])
    hops = 2 * (side - 1) + depth
    scratch = dict(
        red=low(*weights.red.shape),
        spa=low(*weights.spa.shape),
        exp=low(*weights.exp.shape),
        squ=low(*weights.squ.shape),
        mot=low(*weights.mot.shape),
        con=low(*weights.con.shape),
        gat=low(*weights.gat.shape),
        bias=wide(2, *bias.shape),
        norm=wide(2, *norm.shape),
        stage=low(2, *frames.shape[1:]),
        v=low(full, ch),
        nh1=wide(2, full, mid),
        nh2=wide(2, full, mid),
        nh3=wide(2, full * ch // ROW, ROW),
        gs=wide(full * ch // ROW, ROW),
        sigma=wide(2, full, mid),
        a1=low(2, full, mid),
        h2=low(2, full, mid),
        gated=low(2, full, mid),
        field=low(2, full, red_w),
        score=low(2, full, red_w),
        cmean=wide(2, segs, red_w),
        ssum=wide(segs, red_w),
        gbias=wide(1, mid),
        gz3=low(full, ch),
        gz1=low(full, mid),
        gl=low(full, mid),
        gq=low(full, red_w),
        gr=low(full, red_w),
        patch=low(full, 9 * mid),
        patch_m=low(full, 9 * red_w),
        grid=wide(GRID * GRID * segs, mid),
        tmp1=wide(9 * red_w, LANES),
        mix=wide(HALF // LANES, max(parts["spa"][1], parts["exp"][1]), LANES),
        msg=wide(2, len(levels), 2 * ch // LANES, LANES),
        inbox=wide(2, len(levels), group, 2 * ch // LANES, LANES),
        cnt=wide(len(levels), group, 8, LANES),
        total=wide(8, LANES),
        mean=wide(ch // LANES, LANES),
        bsum=wide(2 * ch // LANES, LANES),
        rstd=wide(2, norm_rows // 2, LANES),
        gnorm=wide(2, norm_rows, LANES),
        gnorm_in=wide(norm_rows, LANES),
        g_a=pile_a[0],
        r0_a=pile_a[1],
        r1_a=pile_a[2],
        r2_a=pile_a[3],
        r3_a=pile_a[4],
        g_b=pile_b[0],
        r0_b=pile_b[1],
        r1_b=pile_b[2],
        r2_b=pile_b[3],
        r3_b=pile_b[4],
        g_c=pile_c[0],
        r0_c=pile_c[1],
        r1_c=pile_c[2],
        r2_c=pile_c[3],
        r3_c=pile_c[4],
        fin_red=low(parts["red"][1], HALF),
        fin_spa=low(parts["spa"][1], HALF),
        fin_exp=low(parts["exp"][1], HALF),
        fin_small=low(parts["small"][1], HALF),
        load_sem=sems(2),
        w_sem=sems(len(WEIGHTS)),
        ws_sem=sems(len(WEIGHTS)),
        wr_sem=sems(len(WEIGHTS)),
        p_sem=sems(2),
        ps_sem=sems(2),
        pr_sem=sems(2),
        ms_sem=sems(2, len(levels), group),
        mr_sem=sems(2, len(levels), group),
        cs_sem=sems(len(levels), group),
        cr_sem=sems(len(levels), group),
        o_sem=sems(4, 3),
        rs_send=sems(3, hops),
        rs_recv=sems(3, hops),
        fin_sem=sems(4, pp.reach),
        land_sem=sems(4, 2, PIECES),
        gn_sem=sems(2),
    )
    names = list(ins) + list(outs) + list(scratch)
    results = pl.pallas_call(
        functools.partial(kernel, n, sizes, names),
        out_shape=list(outs.values()),
        in_specs=in_specs,
        out_specs=out_specs,
        scratch_shapes=list(scratch.values()),
        cost_estimate=pl.CostEstimate(
            flops=22 * 10**9, bytes_accessed=10**8, transcendentals=10**7
        ),
        compiler_params=pltpu.CompilerParams(
            collective_id=0, has_side_effects=True, vmem_limit_bytes=64 * 2**20 - 2**17
        ),
    )(*ins.values())
    return results[0], results[1], results[2], results[-1]


def on_device(n, share, frames, out_grad, seg_counts, *params):
    reducer, spatial, expander, squeezer, motion, context, gating, bias, norm = params
    _, segs, pixels, ch = frames.shape
    mid, red_w = reducer.shape[-1], squeezer.shape[-1]
    sizes = (ch, mid, red_w, segs, share)
    weights = SimpleNamespace(
        red=reducer[0],
        spa=spatial[0].transpose(1, 0, 2).reshape(9 * mid, mid),
        exp=expander[0],
        squ=squeezer[0],
        mot=motion[0].transpose(1, 0, 2).reshape(9 * red_w, red_w),
        con=context[0],
        gat=gating[0],
    )
    out, ing, land, gnorm = run(
        n,
        sizes,
        frames.transpose(0, 2, 1, 3),
        out_grad.transpose(0, 2, 1, 3),
        seg_counts,
        weights,
        bias,
        norm[0],
    )
    pp = plan(n, ch, mid, red_w, segs, share)
    start = pp.margin * ROW + lax.rem(lax.axis_index("dp") * share, ROW * 16)
    flat = lax.dynamic_slice(land.astype(F32).reshape(-1), (start,), (share,))
    return (
        out.transpose(0, 2, 1, 3)[None],
        ing.transpose(0, 2, 1, 3)[None],
        flat[None],
        gnorm.reshape(norm.shape),
    )


def solution(mesh):
    n = mesh.shape["dp"]

    def whole(*args):
        entries = sum(item.size // item.shape[0] for item in args[3:11])
        share = up(entries, n) // n
        body = jax.shard_map(
            functools.partial(on_device, n, share),
            mesh=mesh,
            in_specs=(
                P("dp", None, None, None),
                P("dp", None, None, None),
                P("dp"),
                P("pipe", None, None),
                P("pipe", None, None, None),
                P("pipe", None, None),
                P("pipe", None, None),
                P("pipe", None, None, None),
                P("pipe", None, None),
                P("pipe", None, None),
                P("pipe", None),
                P("pipe", None, None),
            ),
            out_specs=(
                P("pipe", "dp", None, None, None),
                P("pipe", "dp", None, None, None),
                P("pipe", "dp"),
                P("pipe", None, None),
            ),
            check_vma=False,
        )
        return body(*args)

    return whole
```

time: 2700 us -> 263 us (0.10)
  blocking collectives: 1130 us -> 0 us
  local copies, waits for them, and re-layouts: 690 us -> 13.8 us
  waiting for transfers between devices: 486 us -> 0 us
  Pallas kernels: 0 us -> 247 us
  matrix products: 177 us -> 0 us
  other arithmetic: 173 us -> 1.6 us
    psum x27 -> x0, blocking collectives: 1130 us -> none  [the longest x9 443 us: norm_backward(): lax.psum((jnp.sum(grad_out, axis=(0, 1)), jnp.sum(grad_out * normed, axis...]
    unnamed x2 -> x0, waiting for transfers between devices: 486 us -> none
    pallas_call x0 -> x1, Pallas kernels: none -> 247 us  [run(): pl.pallas_call(functools.partial(kernel, n, sizes, names), out_shape=list...]
    slice x119 -> x0, local copies, waits for them, and re-layouts: 182 us -> none  [the longest x108 167 us: make_patches(): padded[:, down:down + SIDE, right:right + SIDE, :]]
    dot_general x63 -> x0, matrix products: 177 us -> none  [the longest x3 22.5 us: section_backward(): jnp.einsum('po,cko->pkc', spatial_rows, spatial, preferred_element_type=j...]
    unnamed x685 -> x7, local copies, waits for them, and re-layouts: 182 us -> 6.49 us
    another operation x122 -> x0, local copies, waits for them, and re-layouts: 168 us -> none  [the longest x120 166 us: make_patches(): jnp.stack([padded[:, down:down + SIDE, right:right + SIDE, :] for down in...]
    reshape x14 -> x1, local copies, waits for them, and re-layouts: 58.2 us -> 0.62 us  [on_device(): gnorm.reshape(norm.shape)]
  transfers between devices with their start and end apart: 5 -> 0, of which waited for: 1 -> 0; matrix products, arithmetic and copies ran while one was open for 11% -> 0% of each run, Pallas kernels for 0% -> 0%
where the time goes in v1:
time: 263 us
  Pallas kernels  247 us (94%)
  local copies, waits for them, and re-layouts  13.8 us (5%)
    pallas_call x1, Pallas kernels, run(): pl.pallas_call(functools.partial(kernel, n, sizes, names), out_shape=list...  247 us
    unnamed x7, local copies, waits for them, and re-layouts  6.49 us
    broadcast_in_dim x1, local copies, waits for them, and re-layouts, on_device(): flat[None]  6.31 us

profile of v1, /device:TPU:4, one launch (start us, length us, event | category | flops | bytes accessed | tf_op | source)
XLA Modules:
  0.0 262.9 jit_solution(8125221376137596710)
XLA Ops:
  0.6 246.8 %shard_map.147 = (bf16[2,49,8,2048]{3,2,1,0:T(8,128)(2,1)}, bf16[2,49,8,2048]{3,2,1,0:T(8,128)(2,1)}, bf16[1184,512]{1,0:T(8,128)(2,1)}, bf16[2048,512]{1,0:T(8,...) custom-call(bf16[2,49,8,2048]{3,2,1,0:T(8,128)(2,1)} %bitcast.31, ...), custom_call_target="tpu_custom_call" | custom-call | flops 22000001024 | bytes 100000000 | tf_op jit(solution)/shard_map/pallas_call | solution.py:1220
  247.4 1.6 convert_bitcast_fusion
  249.1 0.6 copy.16
  249.7 0.0 copy-start.1
  249.7 0.4 dynamic_slice.3
  250.1 6.3 %broadcast_in_dim.11 = f32[1,296992]{1,0:T(1,128)} reshape(f32[296992]{0:T(1024)S(1)} %dynamic_slice.3) | data formatting | bytes 2375936 | tf_op jit(solution)/shard_map/broadcast_in_dim | solution.py:1266
  256.4 0.0 copy-done.1
  256.4 0.6 reshape.27
  257.0 0.0 copy-start
  257.0 4.2 %copy.19 = bf16[1,2,8,49,2048]{4,2,3,1,0:T(8,128)(2,1)} copy(bf16[1,2,8,49,2048]{4,2,3,1,0:T(8,128)(2,1)} %bitcast.29) | data formatting | bytes 6422528
  261.2 0.0 copy-done
  261.2 1.7 copy.20
Async XLA Ops:
  249.7 6.7 %copy-start.1 = (f32[48,128]{1,0:T(8,128)S(1)}, f32[48,128]{1,0:T(8,128)}, u32[]{:S(2)}) copy-start(f32[48,128]{1,0:T(8,128)} %get-tuple-element.11) | copy-start | bytes 73732
  257.0 4.2 %copy-start = (bf16[2,49,8,2048]{3,2,1,0:T(8,128)(2,1)S(1)}, bf16[2,49,8,2048]{3,2,1,0:T(8,128)(2,1)}, u32[]{:S(2)}) copy-start(bf16[2,49,8,2048]{3,2,1,0:T(8,128)(2,1)} %get-tuple-element.9) | copy-start | bytes 9633796
